TPU v7x, 512 devices: a whole 4x4x16 slice. The times are simulated.
512 devices in a mesh: ctx: 32 (over y, z_lo), tp: 16 (over x, z_hi, core).
Axes of the slice: x: 4, y: 4, z: 16 (z_hi: 2, z_lo: 8; z = z_hi * 8 + z_lo), core: 2. Of those that a mesh axis runs over, the one named last changes fastest.
Arguments:
- tokens: bfloat16 [4096, 8192], P('ctx', 'tp'), may hold values from -6 to 6
- cotangent: bfloat16 [4096, 8192], P('ctx', 'tp'), may hold values from -6 to 6
- filters: bfloat16 [4096, 8192], P('ctx', 'tp'), may hold values from -0.09375 to 0.09375
Outputs:
- outputs: bfloat16 [4096, 8192], P('ctx', 'tp')
- input_grad: bfloat16 [4096, 8192], P('ctx', 'tp')
All inputs are finite; a program needn't handle non-finite values.
Results may differ from a plain program's by a relative error of at most 0.012.
Values may be sent and summed in bfloat16 or wider, within the bound.
No kernel may reach another device: no remote copies, remote signals or barrier semaphores. Data moves between devices by JAX's collectives and lax.ppermute only.
A program may use at most 64 MiB of HBM per device.

v0:
```python
import math

import jax
import jax.numpy as jnp
import numpy as np
from jax import lax
from jax.experimental import pallas as pl
from jax.experimental.pallas import tpu as pltpu
from jax.sharding import Mesh
from jax.sharding import PartitionSpec as P

LANES = 128
BLOCKS = 32
TOTAL = 2 * LANES * BLOCKS
CH = 8
PARAMS = pltpu.CompilerParams(vmem_limit_bytes=40 * 2**20)


def tables():
    q = np.arange(BLOCKS)[:, None]
    m = np.arange(LANES)[None, :]
    turn = 2.0 * math.pi * (2 * q + 0.5) * m / TOTAL
    lane = np.arange(LANES)
    phase = 2.0 * math.pi * (lane[:, None] * lane[None, :] % LANES) / LANES
    cos, sin = np.cos(phase), np.sin(phase)
    ahead = np.block([[cos, -sin], [sin, cos]]).astype(np.float32)
    halves = []
    for matrix in (ahead, ahead.T):
        high = matrix.astype(jnp.bfloat16)
        low = (matrix - high.astype(np.float32)).astype(jnp.bfloat16)
        halves += [high, low]
    return np.cos(turn).astype(np.float32), np.sin(turn).astype(np.float32), np.stack(halves)


def rotate(value, angle):
    re, im = value
    eighth = round(angle / (math.pi / 4), 9) % 8
    root = math.sqrt(0.5)
    if eighth == 0:
        return re, im
    if eighth == 2:
        return -im, re
    if eighth == 4:
        return -re, -im
    if eighth == 6:
        return im, -re
    if eighth in (1, 3, 5, 7):
        plus, minus = (re + im) * root, (re - im) * root
        return {1: (minus, plus), 3: (-plus, minus), 5: (-minus, -plus), 7: (plus, -minus)}[eighth]
    cos, sin = math.cos(angle), math.sin(angle)
    return re * cos - im * sin, re * sin + im * cos


def dft(values, sign):
    size = len(values)
    if size == 1:
        return values
    if size == 2:
        (ar, ai), (br, bi) = values
        return [(ar + br, ai + bi), (ar - br, ai - bi)]
    radix = 4
    if size % 4 or size == 8:
        radix = 2
    rest = size // radix
    parts = [dft(values[i::radix], sign) for i in range(radix)]
    out = [None] * size
    for k in range(rest):
        turned = [rotate(parts[i][k], sign * 2.0 * math.pi * i * k / size) for i in range(radix)]
        if radix == 2:
            (ar, ai), (br, bi) = turned
            out[k], out[k + rest] = (ar + br, ai + bi), (ar - br, ai - bi)
        else:
            (ar, ai), (br, bi), (cr, ci), (dr, di) = turned
            er, ei, fr, fi = ar + cr, ai + ci, ar - cr, ai - ci
            gr, gi, hr, hi = br + dr, bi + di, (br - dr) * sign, (bi - di) * sign
            out[k] = er + gr, ei + gi
            out[k + rest] = fr - hi, fi + hr
            out[k + 2 * rest] = er - gr, ei - gi
            out[k + 3 * rest] = fr + hi, fi - hr
    return out


def product(left, matrix_high, matrix_low):
    high = left.astype(jnp.bfloat16)
    low = (left - high.astype(jnp.float32)).astype(jnp.bfloat16)
    dot = lambda a, b: jnp.dot(a, b, preferred_element_type=jnp.float32)
    return dot(high, matrix_high) + (dot(low, matrix_high) + dot(high, matrix_low))


def gather_kernel(tok_ref, grad_ref, filt_ref, out_ref):
    for pair in range(out_ref.shape[0] // (6 * CH)):
        if pair % 8 == 0:
            cols = pl.ds(pair * 2 * CH, LANES)
            turned = [ref[:, cols].astype(jnp.float32).T for ref in (tok_ref, grad_ref, filt_ref)]
        at = (pair % 8) * 2 * CH
        rows = [part[at + CH * i : at + CH * (i + 1)] for i in range(2) for part in turned]
        out_ref[pl.ds(pair * 6 * CH, 6 * CH), :] = jnp.concatenate(rows).astype(jnp.bfloat16)


def scatter_kernel(in_ref, out_ref, grad_ref):
    for block in range(out_ref.shape[1] // LANES):
        rows = LANES // CH
        held = in_ref[pl.ds(block * 2 * LANES, 2 * LANES), :].astype(jnp.float32)
        held = held.reshape(rows, 2, CH, LANES)
        for i, ref in enumerate((out_ref, grad_ref)):
            part = held[:, i].reshape(LANES, LANES).T
            ref[:, pl.ds(block * LANES, LANES)] = part.astype(jnp.bfloat16)


def operator_kernel(in_ref, cos_ref, sin_ref, mat_ref, out_ref, work, spec):
    for half in range(2):
        slabs = []
        for n in range(BLOCKS):
            held = in_ref[pl.ds(n * 6 * CH, 6 * CH), :].astype(jnp.float32)
            slabs.append(held[half * 3 * CH : (half + 1) * 3 * CH])
        for a in range(3):
            twisted = []
            for n in range(BLOCKS):
                part = slabs[n][a * CH : (a + 1) * CH]
                angle = math.pi * n / (2 * BLOCKS)
                twisted.append((part * math.cos(angle), part * -math.sin(angle)))
            for q, (re, im) in enumerate(dft(twisted, -1)):
                cos, sin = cos_ref[q : q + 1, :], sin_ref[q : q + 1, :]
                rows = pl.ds((q * 2 + half) * CH, CH)
                work[a, rows, :LANES] = re * cos + im * sin
                work[a, rows, LANES:] = im * cos - re * sin
    for a in range(3):
        spec[a] = product(work[a], mat_ref[0], mat_ref[1])
    step = 8 * CH
    for at in range(0, 2 * BLOCKS * CH, step):
        rows = pl.ds(at, step)
        tok_re, tok_im = spec[0, rows, :LANES], spec[0, rows, LANES:]
        grad_re, grad_im = spec[1, rows, :LANES], spec[1, rows, LANES:]
        filt_re, filt_im = spec[2, rows, :LANES], spec[2, rows, LANES:]
        swap = lambda x: jnp.concatenate(
            [x[(i ^ 1) * CH : (i ^ 1) * CH + CH] for i in range(step // CH)]
        )
        both_re = filt_re + swap(filt_re)
        both_im = filt_im - swap(filt_im)
        work[0, rows, :LANES] = both_re * tok_re - both_im * tok_im
        work[0, rows, LANES:] = both_re * tok_im + both_im * tok_re
        work[1, rows, :LANES] = both_re * grad_re + both_im * grad_im
        work[1, rows, LANES:] = both_re * grad_im - both_im * grad_re
    for a in range(2):
        spec[a] = product(work[a], mat_ref[2], mat_ref[3])
    for half in range(2):
        results = []
        for a in range(2):
            turned = []
            for q in range(BLOCKS):
                cos, sin = cos_ref[q : q + 1, :], sin_ref[q : q + 1, :]
                rows = pl.ds((q * 2 + half) * CH, CH)
                re, im = spec[a, rows, :LANES], spec[a, rows, LANES:]
                turned.append((re * cos - im * sin, re * sin + im * cos))
            made = []
            for n, (re, im) in enumerate(dft(turned, 1)):
                angle = math.pi * n / (2 * BLOCKS)
                scale = 2.0 / TOTAL
                made.append(re * (math.cos(angle) * scale) - im * (math.sin(angle) * scale))
            results.append(made)
        for n in range(BLOCKS):
            rows = pl.ds((n * 2 + half) * 2 * CH, 2 * CH)
            out_ref[rows, :] = jnp.concatenate([r[n] for r in results]).astype(jnp.bfloat16)


def body(tokens, cotangent, filters):
    cos, sin, matrices = tables()
    chans = tokens.shape[1]
    group = ("ctx", "half")
    vmem = pl.BlockSpec(memory_space=pltpu.VMEM)
    sent = pl.pallas_call(
        gather_kernel,
        out_shape=jax.ShapeDtypeStruct((3 * chans, LANES), jnp.bfloat16),
        in_specs=[vmem] * 3,
        out_specs=vmem,
        compiler_params=PARAMS,
    )(tokens, cotangent, filters)
    held = lax.all_to_all(sent, group, split_axis=0, concat_axis=0, tiled=True)
    made = pl.pallas_call(
        operator_kernel,
        out_shape=jax.ShapeDtypeStruct((2 * chans, LANES), jnp.bfloat16),
        in_specs=[vmem] * 4,
        out_specs=vmem,
        scratch_shapes=[
            pltpu.VMEM((3, 2 * BLOCKS * CH, 2 * LANES), jnp.float32),
            pltpu.VMEM((3, 2 * BLOCKS * CH, 2 * LANES), jnp.float32),
        ],
        compiler_params=PARAMS,
    )(held, cos, sin, matrices)
    back = lax.all_to_all(made, group, split_axis=0, concat_axis=0, tiled=True)
    return pl.pallas_call(
        scatter_kernel,
        out_shape=[jax.ShapeDtypeStruct((LANES, chans), jnp.bfloat16)] * 2,
        in_specs=[vmem],
        out_specs=[vmem] * 2,
        compiler_params=PARAMS,
    )(back)


def solution(mesh):
    halves = Mesh(mesh.devices.reshape(BLOCKS, 2, -1), ("ctx", "half", "rest"))
    placed = P("ctx", ("half", "rest"))
    return jax.shard_map(
        body,
        mesh=halves,
        in_specs=(placed,) * 3,
        out_specs=(placed,) * 2,
        check_vma=False,
    )
```

profile of v0, /device:TPU:2, one launch (start us, length us, event | category | flops | bytes accessed | tf_op | source)
XLA Modules:
  0.0 78.8 jit_solution(14254321721685635283)
XLA Ops:
  0.6 0.0 copy-start.1
  0.6 0.9 %copy-done.1 = bf16[128,512]{1,0:T(8,128)(2,1)S(1)} copy-done((bf16[128,512]{1,0:T(8,128)(2,1)S(1)}, bf16[128,512]{1,0:T(8,128)(2,1)}, u32[]{:S(2)}) %copy-start.1) | copy-done | bytes 131096
  1.5 0.0 copy-start.2
  1.5 0.9 %copy-done.2 = bf16[128,512]{1,0:T(8,128)(2,1)S(1)} copy-done((bf16[128,512]{1,0:T(8,128)(2,1)S(1)}, bf16[128,512]{1,0:T(8,128)(2,1)}, u32[]{:S(2)}) %copy-start.2) | copy-done | bytes 131096
  2.4 0.0 copy-start.3
  2.4 0.9 %copy-done.3 = bf16[128,512]{1,0:T(8,128)(2,1)S(1)} copy-done((bf16[128,512]{1,0:T(8,128)(2,1)S(1)}, bf16[128,512]{1,0:T(8,128)(2,1)}, u32[]{:S(2)}) %copy-start.3) | copy-done | bytes 131096
  3.3 0.2 shard_map.77
  3.5 0.0 copy-start
  3.5 0.0 copy-start.4
  3.5 0.0 copy-start.5
  3.6 44.3 %all_to_all.22 = bf16[64,24,128]{2,1,0:T(8,128)(2,1)S(1)} all-to-all(bf16[64,24,128]{2,1,0:T(8,128)(2,1)S(1)} %bitcast.4), channel_id=1, replica_groups=mesh['ctx'=32,'half'=2,'rest'=8] {'ctx','half'}, dimensions={0} | all-to-all | bytes 786432 | tf_op jit(solution)/shard_map/all_to_all | solution.py:178
  47.8 0.0 copy-done
  47.8 0.0 copy-done.4
  47.8 0.0 copy-done.5
  47.8 2.1 %shard_map.78 = bf16[1024,128]{1,0:T(8,128)(2,1)S(1)} custom-call(bf16[1536,128]{1,0:T(8,128)(2,1)S(1)} %bitcast.5, f32[32,128]{1,0:T(8,128)S(1)} %copy-done.5, f32[32,128]{1,0:T(8,128)S(1)} %copy-done.4, bf16[4,256,256]{2,1,0:T(8,128)(2,1)S(1)} %copy-done), custom_call_target="tpu_custom_call" | custom-call | tf_op jit(solution)/shard_map/pallas_call | solution.py:179
  50.0 28.0 %all_to_all.23 = bf16[64,16,128]{2,1,0:T(8,128)(2,1)S(1)} all-to-all(bf16[64,16,128]{2,1,0:T(8,128)(2,1)S(1)} %bitcast.6), channel_id=1, replica_groups=mesh['ctx'=32,'half'=2,'rest'=8] {'ctx','half'}, dimensions={0} | all-to-all | bytes 524288 | tf_op jit(solution)/shard_map/all_to_all | solution.py:190
  78.0 0.8 %shard_map.79 = (bf16[128,512]{1,0:T(8,128)(2,1)}, bf16[128,512]{1,0:T(8,128)(2,1)}) custom-call(bf16[1024,128]{1,0:T(8,128)(2,1)S(1)} %bitcast.7), custom_call_target="tpu_custom_call" | custom-call | tf_op jit(solution)/shard_map/pallas_call | solution.py:191
Async XLA Ops:
  0.6 0.9 %copy-start.1 = (bf16[128,512]{1,0:T(8,128)(2,1)S(1)}, bf16[128,512]{1,0:T(8,128)(2,1)}, u32[]{:S(2)}) copy-start(bf16[128,512]{1,0:T(8,128)(2,1)} %tok_ref.1) | copy-start | bytes 393220
  1.5 0.9 %copy-start.2 = (bf16[128,512]{1,0:T(8,128)(2,1)S(1)}, bf16[128,512]{1,0:T(8,128)(2,1)}, u32[]{:S(2)}) copy-start(bf16[128,512]{1,0:T(8,128)(2,1)} %grad_ref.1) | copy-start | bytes 393220
  2.4 0.9 %copy-start.3 = (bf16[128,512]{1,0:T(8,128)(2,1)S(1)}, bf16[128,512]{1,0:T(8,128)(2,1)}, u32[]{:S(2)}) copy-start(bf16[128,512]{1,0:T(8,128)(2,1)} %filt_ref.1) | copy-start | bytes 393220
  3.5 44.3 %copy-start = (bf16[4,256,256]{2,1,0:T(8,128)(2,1)S(1)}, bf16[4,256,256]{2,1,0:T(8,128)(2,1)}, u32[]{:S(2)}) copy-start(bf16[4,256,256]{2,1,0:T(8,128)(2,1)} %constant.8.clone.mat_ref) | copy-start | bytes 1572868
  3.5 44.3 %copy-start.4 = (f32[32,128]{1,0:T(8,128)S(1)}, f32[32,128]{1,0:T(8,128)}, u32[]{:S(2)}) copy-start(f32[32,128]{1,0:T(8,128)} %constant.7.clone.sin_ref) | copy-start | bytes 49156
  3.5 44.3 %copy-start.5 = (f32[32,128]{1,0:T(8,128)S(1)}, f32[32,128]{1,0:T(8,128)}, u32[]{:S(2)}) copy-start(f32[32,128]{1,0:T(8,128)} %constant.6.clone.cos_ref) | copy-start | bytes 49156
where the time goes:
time: 79.1 us; the launch traced here: 78.8 us
  blocking collectives  72.3 us (91%)
  Pallas kernels  3.15 us (4%)
  local copies, waits for them, and re-layouts  2.73 us (3%)
    all_to_all x1, blocking collectives, body(): held = lax.all_to_all(sent, group, split_axis=0, concat_axis=0, tiled=True)  44.3 us
    all_to_all x1, blocking collectives, body(): back = lax.all_to_all(made, group, split_axis=0, concat_axis=0, tiled=True)  28 us
    unnamed x12, local copies, waits for them, and re-layouts  2.73 us
    pallas_call x1, Pallas kernels, body(): pl.pallas_call(operator_kernel, out_shape=jax.ShapeDtypeStruct((2 * chans...  2.14 us

commit v1 on v0

--- a/solution.py
+++ b/solution.py
@@ -87,24 +87,34 @@
     return dot(high, matrix_high) + (dot(low, matrix_high) + dot(high, matrix_low))
 
 
-def gather_kernel(tok_ref, grad_ref, filt_ref, out_ref):
+def gather_kernel(tok_hbm, grad_hbm, filt_hbm, out_ref, held, sems):
+    copies = []
+    for i, hbm in enumerate((tok_hbm, grad_hbm, filt_hbm)):
+        copies.append(pltpu.make_async_copy(hbm, held.at[i], sems.at[i]))
+        copies[-1].start()
+    for copy in copies:
+        copy.wait()
     for pair in range(out_ref.shape[0] // (6 * CH)):
         if pair % 8 == 0:
             cols = pl.ds(pair * 2 * CH, LANES)
-            turned = [ref[:, cols].astype(jnp.float32).T for ref in (tok_ref, grad_ref, filt_ref)]
+            turned = [held[i, :, cols].astype(jnp.float32).T for i in range(3)]
         at = (pair % 8) * 2 * CH
         rows = [part[at + CH * i : at + CH * (i + 1)] for i in range(2) for part in turned]
         out_ref[pl.ds(pair * 6 * CH, 6 * CH), :] = jnp.concatenate(rows).astype(jnp.bfloat16)
 
 
-def scatter_kernel(in_ref, out_ref, grad_ref):
-    for block in range(out_ref.shape[1] // LANES):
-        rows = LANES // CH
-        held = in_ref[pl.ds(block * 2 * LANES, 2 * LANES), :].astype(jnp.float32)
-        held = held.reshape(rows, 2, CH, LANES)
-        for i, ref in enumerate((out_ref, grad_ref)):
-            part = held[:, i].reshape(LANES, LANES).T
-            ref[:, pl.ds(block * LANES, LANES)] = part.astype(jnp.bfloat16)
+def scatter_kernel(in_ref, out_hbm, grad_hbm, made, sems):
+    rows = LANES // CH
+    copies = []
+    for i, hbm in enumerate((out_hbm, grad_hbm)):
+        for block in range(hbm.shape[1] // LANES):
+            held = in_ref[pl.ds(block * 2 * LANES, 2 * LANES), :].astype(jnp.float32)
+            part = held.reshape(rows, 2, CH, LANES)[:, i].reshape(LANES, LANES).T
+            made[i, :, pl.ds(block * LANES, LANES)] = part.astype(jnp.bfloat16)
+        copies.append(pltpu.make_async_copy(made.at[i], hbm, sems.at[i]))
+        copies[-1].start()
+    for copy in copies:
+        copy.wait()
 
 
 def operator_kernel(in_ref, cos_ref, sin_ref, mat_ref, out_ref, work, spec):
@@ -168,17 +178,20 @@
     chans = tokens.shape[1]
     group = ("ctx", "half")
     vmem = pl.BlockSpec(memory_space=pltpu.VMEM)
+    hbm = pl.BlockSpec(memory_space=pltpu.HBM)
+    fields = [pltpu.with_memory_space_constraint(x, pltpu.HBM) for x in (tokens, cotangent, filters)]
     sent = pl.pallas_call(
         gather_kernel,
-        out_shape=jax.ShapeDtypeStruct((3 * chans, LANES), jnp.bfloat16),
-        in_specs=[vmem] * 3,
+        out_shape=pltpu.VMEM((3 * chans, LANES), jnp.bfloat16),
+        in_specs=[hbm] * 3,
         out_specs=vmem,
+        scratch_shapes=[pltpu.VMEM((3, LANES, chans), jnp.bfloat16), pltpu.SemaphoreType.DMA((3,))],
         compiler_params=PARAMS,
-    )(tokens, cotangent, filters)
+    )(*fields)
     held = lax.all_to_all(sent, group, split_axis=0, concat_axis=0, tiled=True)
     made = pl.pallas_call(
         operator_kernel,
-        out_shape=jax.ShapeDtypeStruct((2 * chans, LANES), jnp.bfloat16),
+        out_shape=pltpu.VMEM((2 * chans, LANES), jnp.bfloat16),
         in_specs=[vmem] * 4,
         out_specs=vmem,
         scratch_shapes=[
@@ -192,7 +205,8 @@
         scatter_kernel,
         out_shape=[jax.ShapeDtypeStruct((LANES, chans), jnp.bfloat16)] * 2,
         in_specs=[vmem],
-        out_specs=[vmem] * 2,
+        out_specs=[hbm] * 2,
+        scratch_shapes=[pltpu.VMEM((2, LANES, chans), jnp.bfloat16), pltpu.SemaphoreType.DMA((2,))],
         compiler_params=PARAMS,
     )(back)
 

time: 79.1 us -> 77.4 us (0.979)
  local copies, waits for them, and re-layouts: 2.73 us -> 0.02 us
  Pallas kernels: 3.15 us -> 4.19 us
    unnamed x12 -> x6, local copies, waits for them, and re-layouts: 2.73 us -> 0.02 us
    pallas_call x2, Pallas kernels: 2.31 us -> 3.37 us  [the longest x1 2.14 us: body(): pl.pallas_call(operator_kernel, out_shape=pltpu.VMEM((2 * chans, LANES),...]
where the time goes in v1:
time: 77.4 us; the launch traced here: 77.2 us
  blocking collectives  72.3 us (93%)
  Pallas kernels  4.19 us (5%)
    all_to_all x1, blocking collectives, body(): held = lax.all_to_all(sent, group, split_axis=0, concat_axis=0, tiled=True)  44.3 us
    all_to_all x1, blocking collectives, body(): back = lax.all_to_all(made, group, split_axis=0, concat_axis=0, tiled=True)  28 us
    pallas_call x1, Pallas kernels, body(): pl.pallas_call(operator_kernel, out_shape=pltpu.VMEM((2 * chans, LANES),...  2.14 us

profile of v1, /device:TPU:2, one launch (start us, length us, event | category | flops | bytes accessed | tf_op | source)
XLA Modules:
  0.0 77.2 jit_solution(8873333798426471704)
XLA Ops:
  0.6 1.2 %shard_map.77 = bf16[1536,128]{1,0:T(8,128)(2,1)S(1)} custom-call(bf16[128,512]{1,0:T(8,128)(2,1)} %tok_hbm.1, bf16[128,512]{1,0:T(8,128)(2,1)} %grad_hbm.1, bf16[128,512]{1,0:T(8,128)(2,1)} %filt_hbm.1), custom_call_target="tpu_custom_call" | custom-call | tf_op jit(solution)/shard_map/pallas_call | solution.py:183
  1.9 0.0 copy-start
  1.9 0.0 copy-start.1
  1.9 0.0 copy-start.2
  1.9 44.3 %all_to_all.22 = bf16[64,24,128]{2,1,0:T(8,128)(2,1)S(1)} all-to-all(bf16[64,24,128]{2,1,0:T(8,128)(2,1)S(1)} %bitcast.4), channel_id=1, replica_groups=mesh['ctx'=32,'half'=2,'rest'=8] {'ctx','half'}, dimensions={0} | all-to-all | bytes 786432 | tf_op jit(solution)/shard_map/all_to_all | solution.py:191
  46.2 0.0 copy-done
  46.2 0.0 copy-done.1
  46.2 0.0 copy-done.2
  46.2 2.1 %shard_map.78 = bf16[1024,128]{1,0:T(8,128)(2,1)S(1)} custom-call(bf16[1536,128]{1,0:T(8,128)(2,1)S(1)} %bitcast.5, f32[32,128]{1,0:T(8,128)S(1)} %copy-done.2, f32[32,128]{1,0:T(8,128)S(1)} %copy-done.1, bf16[4,256,256]{2,1,0:T(8,128)(2,1)S(1)} %copy-done), custom_call_target="tpu_custom_call" | custom-call | tf_op jit(solution)/shard_map/pallas_call | solution.py:192
  48.3 28.0 %all_to_all.23 = bf16[64,16,128]{2,1,0:T(8,128)(2,1)S(1)} all-to-all(bf16[64,16,128]{2,1,0:T(8,128)(2,1)S(1)} %bitcast.6), channel_id=1, replica_groups=mesh['ctx'=32,'half'=2,'rest'=8] {'ctx','half'}, dimensions={0} | all-to-all | bytes 524288 | tf_op jit(solution)/shard_map/all_to_all | solution.py:203
  76.3 0.8 %shard_map.79 = (bf16[128,512]{1,0:T(8,128)(2,1)}, bf16[128,512]{1,0:T(8,128)(2,1)}) custom-call(bf16[1024,128]{1,0:T(8,128)(2,1)S(1)} %bitcast.7), custom_call_target="tpu_custom_call" | custom-call | tf_op jit(solution)/shard_map/pallas_call | solution.py:204
Async XLA Ops:
  1.9 44.3 %copy-start = (bf16[4,256,256]{2,1,0:T(8,128)(2,1)S(1)}, bf16[4,256,256]{2,1,0:T(8,128)(2,1)}, u32[]{:S(2)}) copy-start(bf16[4,256,256]{2,1,0:T(8,128)(2,1)} %constant.8.clone.mat_ref) | copy-start | bytes 1572868
  1.9 44.3 %copy-start.1 = (f32[32,128]{1,0:T(8,128)S(1)}, f32[32,128]{1,0:T(8,128)}, u32[]{:S(2)}) copy-start(f32[32,128]{1,0:T(8,128)} %constant.7.clone.sin_ref) | copy-start | bytes 49156
  1.9 44.3 %copy-start.2 = (f32[32,128]{1,0:T(8,128)S(1)}, f32[32,128]{1,0:T(8,128)}, u32[]{:S(2)}) copy-start(f32[32,128]{1,0:T(8,128)} %constant.6.clone.cos_ref) | copy-start | bytes 49156

commit v2 on v1

v2 whole, which is shorter than its diff:
```python
import math

import jax
import jax.numpy as jnp
import numpy as np
from jax import lax
from jax.experimental import pallas as pl
from jax.experimental.pallas import tpu as pltpu
from jax.sharding import PartitionSpec as P

LANES = 128
BLOCKS = 32
TOTAL = 2 * LANES * BLOCKS
CH = 8
PART = 128
PARAMS = pltpu.CompilerParams(vmem_limit_bytes=40 * 2**20)


def tables():
    q = np.arange(BLOCKS)[:, None]
    m = np.arange(LANES)[None, :]
    turn = 2.0 * math.pi * (2 * q + 0.5) * m / TOTAL
    lane = np.arange(LANES)
    phase = 2.0 * math.pi * (lane[:, None] * lane[None, :] % LANES) / LANES
    cos, sin = np.cos(phase), np.sin(phase)
    ahead = np.block([[cos, -sin], [sin, cos]]).astype(np.float32)
    halves = []
    for matrix in (ahead, ahead.T):
        high = matrix.astype(jnp.bfloat16)
        low = (matrix - high.astype(np.float32)).astype(jnp.bfloat16)
        halves.append(np.concatenate([high, high, low]))
    return np.cos(turn).astype(np.float32), np.sin(turn).astype(np.float32), np.stack(halves)


def rotate(value, angle):
    re, im = value
    eighth = round(angle / (math.pi / 4), 9) % 8
    root = math.sqrt(0.5)
    if eighth == 0:
        return re, im
    if eighth == 2:
        return -im, re
    if eighth == 4:
        return -re, -im
    if eighth == 6:
        return im, -re
    if eighth in (1, 3, 5, 7):
        plus, minus = (re + im) * root, (re - im) * root
        return {1: (minus, plus), 3: (-plus, minus), 5: (-minus, -plus), 7: (plus, -minus)}[eighth]
    cos, sin = math.cos(angle), math.sin(angle)
    return re * cos - im * sin, re * sin + im * cos


def dft(values, sign):
    size = len(values)
    if size == 1:
        return values
    if size == 2:
        (ar, ai), (br, bi) = values
        return [(ar + br, ai + bi), (ar - br, ai - bi)]
    radix = 4
    if size % 4 or size == 8:
        radix = 2
    rest = size // radix
    parts = [dft(values[i::radix], sign) for i in range(radix)]
    out = [None] * size
    for k in range(rest):
        turned = [rotate(parts[i][k], sign * 2.0 * math.pi * i * k / size) for i in range(radix)]
        if radix == 2:
            (ar, ai), (br, bi) = turned
            out[k], out[k + rest] = (ar + br, ai + bi), (ar - br, ai - bi)
        else:
            (ar, ai), (br, bi), (cr, ci), (dr, di) = turned
            er, ei, fr, fi = ar + cr, ai + ci, ar - cr, ai - ci
            gr, gi, hr, hi = br + dr, bi + di, (br - dr) * sign, (bi - di) * sign
            out[k] = er + gr, ei + gi
            out[k + rest] = fr - hi, fi + hr
            out[k + 2 * rest] = er - gr, ei - gi
            out[k + 3 * rest] = fr + hi, fi - hr
    return out


def product(left, matrix):
    high = left.astype(jnp.bfloat16)
    low = (left - high.astype(jnp.float32)).astype(jnp.bfloat16)
    parts = jnp.concatenate([high, low, high], axis=1)
    return jnp.dot(parts, matrix, preferred_element_type=jnp.float32)


def gather_kernel(tok_hbm, grad_hbm, filt_hbm, out_ref, held, sems):
    copies = []
    for i, hbm in enumerate((tok_hbm, grad_hbm, filt_hbm)):
        copies.append(pltpu.make_async_copy(hbm, held.at[i], sems.at[i]))
        copies[-1].start()
    for copy in copies:
        copy.wait()
    per = LANES // (2 * CH)
    for block in range(held.shape[2] // LANES):
        cols = pl.ds(block * LANES, LANES)
        turned = [held[i, :, cols].astype(jnp.float32).T for i in range(3)]
        for j in range(per):
            rows = [part[2 * CH * j : 2 * CH * (j + 1)] for part in turned]
            at = pl.ds((block * per + j) * 6 * CH, 6 * CH)
            out_ref[at, :] = jnp.concatenate(rows).astype(jnp.bfloat16)


def scatter_kernel(in_ref, out_hbm, grad_hbm, made, sems):
    rows = LANES // (2 * CH)
    copies = []
    for i, hbm in enumerate((out_hbm, grad_hbm)):
        for block in range(hbm.shape[1] // LANES):
            held = in_ref[pl.ds(block * 2 * LANES, 2 * LANES), :].astype(jnp.float32)
            part = held.reshape(rows, 2, 2 * CH, LANES)[:, i].reshape(LANES, LANES).T
            made[i, :, pl.ds(block * LANES, LANES)] = part.astype(jnp.bfloat16)
        copies.append(pltpu.make_async_copy(made.at[i], hbm, sems.at[i]))
        copies[-1].start()
    for copy in copies:
        copy.wait()


def mix(first, second):
    total = max(len(first), 1)
    done = 0
    for i, step in enumerate(first):
        step()
        while done < len(second) * (i + 1) // total:
            second[done]()
            done += 1
    for step in second[done:]:
        step()


def dft_steps(load, sign, store):
    parts = {}

    def inner(i):
        def step():
            parts[i] = dft([load(n) for n in range(i, BLOCKS, 4)], sign)
        return step

    def outer(k):
        def step():
            turned = [rotate(parts[i][k], sign * 2.0 * math.pi * i * k / BLOCKS) for i in range(4)]
            for j, value in enumerate(dft(turned, sign)):
                store(k + 8 * j, value)
        return step

    return [inner(i) for i in range(4)] + [outer(k) for k in range(8)]


def ahead(read, cos_ref, sin_ref, work, slab):
    def load(n):
        part, angle = read(n), math.pi * n / (2 * BLOCKS)
        return part * math.cos(angle), part * -math.sin(angle)

    def store(q, value):
        re, im = value
        cos, sin = cos_ref[q : q + 1, :], sin_ref[q : q + 1, :]
        rows = pl.ds((slab * BLOCKS + q) * CH, CH)
        work[rows, :LANES] = re * cos + im * sin
        work[rows, LANES:] = im * cos - re * sin

    return dft_steps(load, -1, store)


def lanes(work, spec, mat_ref, which, slab):
    def step(at):
        def run():
            rows = pl.ds(slab * BLOCKS * CH + at, PART)
            spec[rows] = product(work[rows], mat_ref[which])

        return run

    return [step(at) for at in range(0, BLOCKS * CH, PART)]


def field_kernel(in_ref, cos_ref, sin_ref, mat_ref, spec, work):
    def steps(a):
        made = []
        for slab in range(2):

            def read(n, slab=slab):
                held = in_ref[pl.ds(n * 6 * CH + a * 2 * CH, 2 * CH), :].astype(jnp.float32)
                return held[slab * CH : (slab + 1) * CH]

            made += ahead(read, cos_ref, sin_ref, work.at[a], slab)
        return made

    inner = lambda a: [s for h in range(2) for s in lanes(work.at[a], spec.at[a], mat_ref, 0, h)]
    mix(steps(0), [])
    mix(steps(1), inner(0))
    mix(steps(2), inner(1))
    mix([], inner(2))


def operator_kernel(in_ref, spec, cos_ref, sin_ref, mat_ref, out_ref, work, other):
    size = BLOCKS * CH

    def steps(slab):
        def read(n):
            held = in_ref[pl.ds(n * 2 * CH, 2 * CH), :].astype(jnp.float32)
            return held[slab * CH : (slab + 1) * CH]

        return ahead(read, cos_ref, sin_ref, work.at[2], slab)

    def multiply(slab):
        def step(at):
            def run():
                rows = pl.ds(slab * size + at, 64)
                re = spec[2, rows, :LANES] + other[2, rows, :LANES]
                im = spec[2, rows, LANES:] - other[2, rows, LANES:]
                for a, turn in enumerate((im, -im)):
                    has_re, has_im = spec[a, rows, :LANES], spec[a, rows, LANES:]
                    work[a, rows, :LANES] = re * has_re - turn * has_im
                    work[a, rows, LANES:] = re * has_im + turn * has_re

            return run

        return [step(at) for at in range(0, size, 64)]

    def back(a, slab):
        def load(q):
            cos, sin = cos_ref[q : q + 1, :], sin_ref[q : q + 1, :]
            rows = pl.ds(slab * size + q * CH, CH)
            re, im = other[a, rows, :LANES], other[a, rows, LANES:]
            return re * cos - im * sin, re * sin + im * cos

        def store(n, value):
            angle, scale = math.pi * n / (2 * BLOCKS), 2.0 / TOTAL
            re, im = value
            part = re * (math.cos(angle) * scale) - im * (math.sin(angle) * scale)
            kept = pl.ds(n * CH, CH)
            if slab == 0:
                work[2, kept, :LANES] = part
            else:
                both = jnp.concatenate([work[2, kept, :LANES], part])
                out_ref[pl.ds((n * 2 + a) * 2 * CH, 2 * CH), :] = both.astype(jnp.bfloat16)

        return dft_steps(load, 1, store)

    inner = lambda a, slab, which: lanes(work.at[a], other.at[a], mat_ref, which, slab)
    mix(steps(0), [])
    mix(steps(1), inner(2, 0, 0))
    mix(multiply(0), inner(2, 1, 0))
    mix(multiply(1), inner(0, 0, 1))
    mix(back(0, 0), inner(0, 1, 1))
    mix(back(0, 1), inner(1, 0, 1))
    mix(back(1, 0), inner(1, 1, 1))
    mix(back(1, 1), [])


def body(tokens, cotangent, filters):
    cos, sin, matrices = tables()
    chans = tokens.shape[1]
    rows = 2 * BLOCKS * CH
    mirror = lax.axis_size("tp") // 2
    vmem = pl.BlockSpec(memory_space=pltpu.VMEM)
    hbm = pl.BlockSpec(memory_space=pltpu.HBM)
    fields = [pltpu.with_memory_space_constraint(x, pltpu.HBM) for x in (tokens, cotangent, filters)]
    sent = pl.pallas_call(
        gather_kernel,
        out_shape=pltpu.VMEM((3 * chans, LANES), jnp.bfloat16),
        in_specs=[hbm] * 3,
        out_specs=vmem,
        scratch_shapes=[pltpu.VMEM((3, LANES, chans), jnp.bfloat16), pltpu.SemaphoreType.DMA((3,))],
        compiler_params=PARAMS,
    )(*fields)
    held = lax.all_to_all(sent, "ctx", split_axis=0, concat_axis=0, tiled=True)
    own = held.reshape(BLOCKS, 3, 2 * CH, LANES)[:, 2].reshape(rows, LANES)
    other = lax.ppermute(own, "tp", [(i, i ^ mirror) for i in range(2 * mirror)])
    spectra = pl.pallas_call(
        field_kernel,
        out_shape=pltpu.VMEM((3, rows, 2 * LANES), jnp.float32),
        in_specs=[vmem] * 4,
        out_specs=vmem,
        scratch_shapes=[pltpu.VMEM((3, rows, 2 * LANES), jnp.float32)],
        compiler_params=PARAMS,
        cost_estimate=pl.CostEstimate(flops=10**9, bytes_accessed=10**6, transcendentals=0),
    )(held, cos, sin, matrices)
    made = pl.pallas_call(
        operator_kernel,
        out_shape=pltpu.VMEM((2 * chans, LANES), jnp.bfloat16),
        in_specs=[vmem] * 5,
        out_specs=vmem,
        scratch_shapes=[pltpu.VMEM((3, rows, 2 * LANES), jnp.float32)] * 2,
        compiler_params=PARAMS,
        cost_estimate=pl.CostEstimate(flops=10**9, bytes_accessed=10**6, transcendentals=0),
    )(other, spectra, cos, sin, matrices)
    back = lax.all_to_all(made, "ctx", split_axis=0, concat_axis=0, tiled=True)
    return pl.pallas_call(
        scatter_kernel,
        out_shape=[jax.ShapeDtypeStruct((LANES, chans), jnp.bfloat16)] * 2,
        in_specs=[vmem],
        out_specs=[hbm] * 2,
        scratch_shapes=[pltpu.VMEM((2, LANES, chans), jnp.bfloat16), pltpu.SemaphoreType.DMA((2,))],
        compiler_params=PARAMS,
    )(back)


def solution(mesh):
    return jax.shard_map(
        body,
        mesh=mesh,
        in_specs=(P("ctx", "tp"),) * 3,
        out_specs=(P("ctx", "tp"),) * 2,
        check_vma=False,
    )
```

time: 77.4 us -> 76.3 us (0.986)
  the two profiles are of different devices: /device:TPU:2 before, /device:TPU:6 now
where the time goes in v2:
time: 76.3 us; the launch traced here: 76 us
  blocking collectives  63.7 us (83%)
  Pallas kernels  4.36 us (6%)
  waiting for transfers between devices  3.88 us (5%)
  starting transfers between devices  3.31 us (4%)
    all_to_all x1, blocking collectives, body(): held = lax.all_to_all(sent, 'ctx', split_axis=0, concat_axis=0, tiled=True)  40.2 us
    all_to_all x1, blocking collectives, body(): back = lax.all_to_all(made, 'ctx', split_axis=0, concat_axis=0, tiled=True)  23.6 us
    ppermute x1, waiting for transfers between devices, body(): lax.ppermute(own, 'tp', [(i, i ^ mirror) for i in range(2 * mirror)])  3.88 us
    ppermute x1, starting transfers between devices, body(): lax.ppermute(own, 'tp', [(i, i ^ mirror) for i in range(2 * mirror)])  3.31 us
  transfers between devices with their start and end apart: 1, of which 1 were waited for; matrix products, arithmetic and copies ran while one was open for 0% of the time, Pallas kernels for 1%

profile of v2, /device:TPU:6, one launch (start us, length us, event | category | flops | bytes accessed | tf_op | source)
XLA Modules:
  0.0 76.0 jit_solution(9642189829685295161)
XLA Ops:
  0.6 0.0 copy-start
  0.6 0.0 copy-start.1
  0.7 0.0 copy-start.2
  0.7 1.3 %shard_map.77 = bf16[1536,128]{1,0:T(8,128)(2,1)S(1)} custom-call(bf16[128,512]{1,0:T(8,128)(2,1)} %tok_hbm.1, bf16[128,512]{1,0:T(8,128)(2,1)} %grad_hbm.1, bf16[128,512]{1,0:T(8,128)(2,1)} %filt_hbm.1), custom_call_target="tpu_custom_call" | custom-call | tf_op jit(solution)/shard_map/pallas_call | solution.py:260
  2.0 40.2 %all_to_all.22 = bf16[32,48,128]{2,1,0:T(8,128)(2,1)S(1)} all-to-all(bf16[32,48,128]{2,1,0:T(8,128)(2,1)S(1)} %bitcast.6), channel_id=1, replica_groups=mesh['ctx'=32,'tp'=16] {'ctx'}, dimensions={0} | all-to-all | bytes 786432 | tf_op jit(solution)/shard_map/all_to_all | solution.py:268
  42.2 3.3 %collective-permute-start = (bf16[512,128]{1,0:T(8,128)(2,1)S(1)}, bf16[512,128]{1,0:T(8,128)(2,1)S(1)}, u32[]{:S(2)}, u32[]{:S(2)}) collective-permute-start(bf16[512,128]{1,0:T(8,128)(2,1)S(1)} %bitcast.11), channel_id=1, source_target_pairs={{0,8},{1,9},{2,10},{3,11},{4,12},{5,13},{6,14},{7,15},{8,0},{9,1},... | collective-permute-start | bytes 393224 | tf_op jit(solution)/shard_map/ppermute | solution.py:270
  45.5 0.0 copy-done
  45.5 0.0 copy-done.1
  45.5 0.0 copy-done.2
  45.5 1.1 %shard_map.78.spec = f32[3,512,256]{2,1,0:T(8,128)S(1)} custom-call(bf16[1536,128]{1,0:T(8,128)(2,1)S(1)} %bitcast.9, f32[32,128]{1,0:T(8,128)S(1)} %copy-done.2, f32[32,128]{1,0:T(8,128)S(1)} %copy-done.1, bf16[2,768,256]{2,1,0:T(8,128)(2,1)S(1)} %copy-done), custom_call_target="tpu_custom_call" | custom-call | flops 1000000000 | bytes 1000000 | tf_op jit(solution)/shard_map/pallas_call | solution.py:271
  46.7 3.9 %collective-permute-done.in_ref = bf16[512,128]{1,0:T(8,128)(2,1)S(1)} collective-permute-done((bf16[512,128]{1,0:T(8,128)(2,1)S(1)}, bf16[512,128]{1,0:T(8,128)(2,1)S(1)}, u32[]{:S(2)}, u32[]{:S(2)}) %collective-permute-start) | collective-permute-done | bytes 131104 | tf_op jit(solution)/shard_map/ppermute | solution.py:270
  50.6 1.1 %shard_map.79 = bf16[1024,128]{1,0:T(8,128)(2,1)S(1)} custom-call(bf16[512,128]{1,0:T(8,128)(2,1)S(1)} %collective-permute-done.in_ref, f32[3,512,256]{2,1,0:T(8,128)S(1)} %shard_map.78.spec, f32[32,128]{1,0:T(8,128)S(1)} %copy-done.2, f32[32,128]{1,0:T(8,128)S(1)} %copy-done.1, bf16[2,768,256]{2,1,0:T(8,128)(2,1)S(1)} %copy-done), custom_call_target="tpu_custom_call" | custom-call | flops 1000000000 | bytes 1000000 | tf_op jit(solution)/shard_map/pallas_call | solution.py:280
  51.7 23.6 %all_to_all.23 = bf16[32,32,128]{2,1,0:T(8,128)(2,1)S(1)} all-to-all(bf16[32,32,128]{2,1,0:T(8,128)(2,1)S(1)} %bitcast.10), channel_id=1, replica_groups=mesh['ctx'=32,'tp'=16] {'ctx'}, dimensions={0} | all-to-all | bytes 524288 | tf_op jit(solution)/shard_map/all_to_all | solution.py:289
  75.2 0.8 %shard_map.80 = (bf16[128,512]{1,0:T(8,128)(2,1)}, bf16[128,512]{1,0:T(8,128)(2,1)}) custom-call(bf16[1024,128]{1,0:T(8,128)(2,1)S(1)} %bitcast.7), custom_call_target="tpu_custom_call" | custom-call | tf_op jit(solution)/shard_map/pallas_call | solution.py:290
  (1 shorter events, 0.0 us)
Async XLA Ops:
  0.6 44.9 %copy-start = (bf16[2,768,256]{2,1,0:T(8,128)(2,1)S(1)}, bf16[2,768,256]{2,1,0:T(8,128)(2,1)}, u32[]{:S(2)}) copy-start(bf16[2,768,256]{2,1,0:T(8,128)(2,1)} %constant.8.clone.mat_ref) | copy-start | bytes 2359300
  0.6 44.9 %copy-start.1 = (f32[32,128]{1,0:T(8,128)S(1)}, f32[32,128]{1,0:T(8,128)}, u32[]{:S(2)}) copy-start(f32[32,128]{1,0:T(8,128)} %constant.7.clone.sin_ref) | copy-start | bytes 49156
  0.7 44.9 %copy-start.2 = (f32[32,128]{1,0:T(8,128)S(1)}, f32[32,128]{1,0:T(8,128)}, u32[]{:S(2)}) copy-start(f32[32,128]{1,0:T(8,128)} %constant.6.clone.cos_ref) | copy-start | bytes 49156
  42.2 8.4 %collective-permute-start = (bf16[512,128]{1,0:T(8,128)(2,1)S(1)}, bf16[512,128]{1,0:T(8,128)(2,1)S(1)}, u32[]{:S(2)}, u32[]{:S(2)}) collective-permute-start(bf16[512,128]{1,0:T(8,128)(2,1)S(1)} %bitcast.11), channel_id=1, source_target_pairs={{0,8},{1,9},{2,10},{3,11},{4,12},{5,13},{6,14},{7,15},{8,0},{9,1},... | collective-permute-start | bytes 393224 | tf_op jit(solution)/shard_map/ppermute | solution.py:270

commit v3 on v2

--- a/solution.py
+++ b/solution.py
@@ -13,6 +13,8 @@
 TOTAL = 2 * LANES * BLOCKS
 CH = 8
 PART = 128
+ORDER = (4, 12, 24, 2, 28, 10, 18, 27, 21, 9, 19, 8, 6, 17, 13, 15, 29, 3, 5, 1, 7, 14, 0, 31, 20, 30, 26, 22, 25, 11, 23, 16)
+PLACE = tuple(ORDER.index(n) for n in range(BLOCKS))
 PARAMS = pltpu.CompilerParams(vmem_limit_bytes=40 * 2**20)
 
 
@@ -100,7 +102,7 @@
         turned = [held[i, :, cols].astype(jnp.float32).T for i in range(3)]
         for j in range(per):
             rows = [part[2 * CH * j : 2 * CH * (j + 1)] for part in turned]
-            at = pl.ds((block * per + j) * 6 * CH, 6 * CH)
+            at = pl.ds(PLACE[block * per + j] * 6 * CH, 6 * CH)
             out_ref[at, :] = jnp.concatenate(rows).astype(jnp.bfloat16)
 
 
@@ -109,8 +111,9 @@
     copies = []
     for i, hbm in enumerate((out_hbm, grad_hbm)):
         for block in range(hbm.shape[1] // LANES):
-            held = in_ref[pl.ds(block * 2 * LANES, 2 * LANES), :].astype(jnp.float32)
-            part = held.reshape(rows, 2, 2 * CH, LANES)[:, i].reshape(LANES, LANES).T
+            spots = [(PLACE[block * rows + j] * 2 + i) * 2 * CH for j in range(rows)]
+            held = [in_ref[pl.ds(at, 2 * CH), :].astype(jnp.float32) for at in spots]
+            part = jnp.concatenate(held).T
             made[i, :, pl.ds(block * LANES, LANES)] = part.astype(jnp.bfloat16)
         copies.append(pltpu.make_async_copy(made.at[i], hbm, sems.at[i]))
         copies[-1].start()
@@ -180,7 +183,7 @@
         for slab in range(2):
 
             def read(n, slab=slab):
-                held = in_ref[pl.ds(n * 6 * CH + a * 2 * CH, 2 * CH), :].astype(jnp.float32)
+                held = in_ref[pl.ds((PLACE[n] * 3 + a) * 2 * CH, 2 * CH), :].astype(jnp.float32)
                 return held[slab * CH : (slab + 1) * CH]
 
             made += ahead(read, cos_ref, sin_ref, work.at[a], slab)
@@ -198,7 +201,7 @@
 
     def steps(slab):
         def read(n):
-            held = in_ref[pl.ds(n * 2 * CH, 2 * CH), :].astype(jnp.float32)
+            held = in_ref[pl.ds(PLACE[n] * 2 * CH, 2 * CH), :].astype(jnp.float32)
             return held[slab * CH : (slab + 1) * CH]
 
         return ahead(read, cos_ref, sin_ref, work.at[2], slab)
@@ -234,7 +237,7 @@
                 work[2, kept, :LANES] = part
             else:
                 both = jnp.concatenate([work[2, kept, :LANES], part])
-                out_ref[pl.ds((n * 2 + a) * 2 * CH, 2 * CH), :] = both.astype(jnp.bfloat16)
+                out_ref[pl.ds((PLACE[n] * 2 + a) * 2 * CH, 2 * CH), :] = both.astype(jnp.bfloat16)
 
         return dft_steps(load, 1, store)
 
@@ -247,6 +250,12 @@
     mix(back(0, 1), inner(1, 0, 1))
     mix(back(1, 0), inner(1, 1, 1))
     mix(back(1, 1), [])
+
+
+def exchange(rows):
+    return lax.all_to_all(
+        rows, "ctx", split_axis=0, concat_axis=0, tiled=True, axis_index_groups=[list(ORDER)]
+    )
 
 
 def body(tokens, cotangent, filters):
@@ -265,7 +274,7 @@
         scratch_shapes=[pltpu.VMEM((3, LANES, chans), jnp.bfloat16), pltpu.SemaphoreType.DMA((3,))],
         compiler_params=PARAMS,
     )(*fields)
-    held = lax.all_to_all(sent, "ctx", split_axis=0, concat_axis=0, tiled=True)
+    held = exchange(sent)
     own = held.reshape(BLOCKS, 3, 2 * CH, LANES)[:, 2].reshape(rows, LANES)
     other = lax.ppermute(own, "tp", [(i, i ^ mirror) for i in range(2 * mirror)])
     spectra = pl.pallas_call(
@@ -286,7 +295,7 @@
         compiler_params=PARAMS,
         cost_estimate=pl.CostEstimate(flops=10**9, bytes_accessed=10**6, transcendentals=0),
     )(other, spectra, cos, sin, matrices)
-    back = lax.all_to_all(made, "ctx", split_axis=0, concat_axis=0, tiled=True)
+    back = exchange(made)
     return pl.pallas_call(
         scatter_kernel,
         out_shape=[jax.ShapeDtypeStruct((LANES, chans), jnp.bfloat16)] * 2,

time: 76.3 us -> 65.7 us (0.86)
  blocking collectives: 63.7 us -> 53.1 us
    all_to_all x2, blocking collectives: 63.7 us -> 53.1 us  [exchange(): lax.all_to_all(rows, 'ctx', split_axis=0, concat_axis=0, tiled=True, axis...]
  transfers between devices with their start and end apart: 1 -> 1, of which waited for: 1 -> 1; matrix products, arithmetic and copies ran while one was open for 0% -> 0% of each run, Pallas kernels for 1% -> 2%
where the time goes in v3:
time: 65.7 us; the launch traced here: 65.4 us
  blocking collectives  53.1 us (81%)
  Pallas kernels  4.38 us (7%)
  waiting for transfers between devices  3.88 us (6%)
  starting transfers between devices  3.31 us (5%)
  between operations  0.71 us (1%)
    all_to_all x2, blocking collectives, exchange(): lax.all_to_all(rows, 'ctx', split_axis=0, concat_axis=0, tiled=True, axis...  53.1 us
    ppermute x1, waiting for transfers between devices, body(): lax.ppermute(own, 'tp', [(i, i ^ mirror) for i in range(2 * mirror)])  3.88 us
    ppermute x1, starting transfers between devices, body(): lax.ppermute(own, 'tp', [(i, i ^ mirror) for i in range(2 * mirror)])  3.31 us
  transfers between devices with their start and end apart: 1, of which 1 were waited for; matrix products, arithmetic and copies ran while one was open for 0% of the time, Pallas kernels for 2%

profile of v3, /device:TPU:6, one launch (start us, length us, event | category | flops | bytes accessed | tf_op | source)
XLA Modules:
  0.0 65.4 jit_solution(4308594879032528697)
XLA Ops:
  0.6 0.0 copy-start
  0.6 0.0 copy-start.1
  0.7 0.0 copy-start.2
  0.7 1.3 %shard_map.77 = bf16[1536,128]{1,0:T(8,128)(2,1)S(1)} custom-call(bf16[128,512]{1,0:T(8,128)(2,1)} %tok_hbm.1, bf16[128,512]{1,0:T(8,128)(2,1)} %grad_hbm.1, bf16[128,512]{1,0:T(8,128)(2,1)} %filt_hbm.1), custom_call_target="tpu_custom_call" | custom-call | tf_op jit(solution)/shard_map/pallas_call | solution.py:269
  2.0 34.8 %all_to_all.22 = bf16[32,48,128]{2,1,0:T(8,128)(2,1)S(1)} all-to-all(bf16[32,48,128]{2,1,0:T(8,128)(2,1)S(1)} %bitcast.6), channel_id=1, replica_groups={{64,192,384,32,448,160,288,432,336,144,304,128,96,272,208,240,464,48,80..., dimensions={0} | all-to-all | bytes 786432 | tf_op jit(solution)/shard_map/all_to_all | solution.py:256
  36.7 3.3 %collective-permute-start = (bf16[512,128]{1,0:T(8,128)(2,1)S(1)}, bf16[512,128]{1,0:T(8,128)(2,1)S(1)}, u32[]{:S(2)}, u32[]{:S(2)}) collective-permute-start(bf16[512,128]{1,0:T(8,128)(2,1)S(1)} %bitcast.11), channel_id=1, source_target_pairs={{0,8},{1,9},{2,10},{3,11},{4,12},{5,13},{6,14},{7,15},{8,0},{9,1},... | collective-permute-start | bytes 393224 | tf_op jit(solution)/shard_map/ppermute | solution.py:279
  40.1 0.0 copy-done
  40.1 0.0 copy-done.1
  40.1 0.0 copy-done.2
  40.1 1.1 %shard_map.78.spec = f32[3,512,256]{2,1,0:T(8,128)S(1)} custom-call(bf16[1536,128]{1,0:T(8,128)(2,1)S(1)} %bitcast.9, f32[32,128]{1,0:T(8,128)S(1)} %copy-done.2, f32[32,128]{1,0:T(8,128)S(1)} %copy-done.1, bf16[2,768,256]{2,1,0:T(8,128)(2,1)S(1)} %copy-done), custom_call_target="tpu_custom_call" | custom-call | flops 1000000000 | bytes 1000000 | tf_op jit(solution)/shard_map/pallas_call | solution.py:280
  41.2 3.9 %collective-permute-done.in_ref = bf16[512,128]{1,0:T(8,128)(2,1)S(1)} collective-permute-done((bf16[512,128]{1,0:T(8,128)(2,1)S(1)}, bf16[512,128]{1,0:T(8,128)(2,1)S(1)}, u32[]{:S(2)}, u32[]{:S(2)}) %collective-permute-start) | collective-permute-done | bytes 131104 | tf_op jit(solution)/shard_map/ppermute | solution.py:279
  45.1 1.1 %shard_map.79 = bf16[1024,128]{1,0:T(8,128)(2,1)S(1)} custom-call(bf16[512,128]{1,0:T(8,128)(2,1)S(1)} %collective-permute-done.in_ref, f32[3,512,256]{2,1,0:T(8,128)S(1)} %shard_map.78.spec, f32[32,128]{1,0:T(8,128)S(1)} %copy-done.2, f32[32,128]{1,0:T(8,128)S(1)} %copy-done.1, bf16[2,768,256]{2,1,0:T(8,128)(2,1)S(1)} %copy-done), custom_call_target="tpu_custom_call" | custom-call | flops 1000000000 | bytes 1000000 | tf_op jit(solution)/shard_map/pallas_call | solution.py:289
  46.3 18.4 %all_to_all.23 = bf16[32,32,128]{2,1,0:T(8,128)(2,1)S(1)} all-to-all(bf16[32,32,128]{2,1,0:T(8,128)(2,1)S(1)} %bitcast.10), channel_id=1, replica_groups={{64,192,384,32,448,160,288,432,336,144,304,128,96,272,208,240,464,48,80..., dimensions={0} | all-to-all | bytes 524288 | tf_op jit(solution)/shard_map/all_to_all | solution.py:256
  64.6 0.8 %shard_map.80 = (bf16[128,512]{1,0:T(8,128)(2,1)}, bf16[128,512]{1,0:T(8,128)(2,1)}) custom-call(bf16[1024,128]{1,0:T(8,128)(2,1)S(1)} %bitcast.7), custom_call_target="tpu_custom_call" | custom-call | tf_op jit(solution)/shard_map/pallas_call | solution.py:299
  (1 shorter events, 0.0 us)
Async XLA Ops:
  0.6 39.4 %copy-start = (bf16[2,768,256]{2,1,0:T(8,128)(2,1)S(1)}, bf16[2,768,256]{2,1,0:T(8,128)(2,1)}, u32[]{:S(2)}) copy-start(bf16[2,768,256]{2,1,0:T(8,128)(2,1)} %constant.8.clone.mat_ref) | copy-start | bytes 2359300
  0.6 39.4 %copy-start.1 = (f32[32,128]{1,0:T(8,128)S(1)}, f32[32,128]{1,0:T(8,128)}, u32[]{:S(2)}) copy-start(f32[32,128]{1,0:T(8,128)} %constant.7.clone.sin_ref) | copy-start | bytes 49156
  0.7 39.4 %copy-start.2 = (f32[32,128]{1,0:T(8,128)S(1)}, f32[32,128]{1,0:T(8,128)}, u32[]{:S(2)}) copy-start(f32[32,128]{1,0:T(8,128)} %constant.6.clone.cos_ref) | copy-start | bytes 49156
  36.7 8.4 %collective-permute-start = (bf16[512,128]{1,0:T(8,128)(2,1)S(1)}, bf16[512,128]{1,0:T(8,128)(2,1)S(1)}, u32[]{:S(2)}, u32[]{:S(2)}) collective-permute-start(bf16[512,128]{1,0:T(8,128)(2,1)S(1)} %bitcast.11), channel_id=1, source_target_pairs={{0,8},{1,9},{2,10},{3,11},{4,12},{5,13},{6,14},{7,15},{8,0},{9,1},... | collective-permute-start | bytes 393224 | tf_op jit(solution)/shard_map/ppermute | solution.py:279

commit v4 on v3

--- a/solution.py
+++ b/solution.py
@@ -13,8 +13,10 @@
 TOTAL = 2 * LANES * BLOCKS
 CH = 8
 PART = 128
-ORDER = (4, 12, 24, 2, 28, 10, 18, 27, 21, 9, 19, 8, 6, 17, 13, 15, 29, 3, 5, 1, 7, 14, 0, 31, 20, 30, 26, 22, 25, 11, 23, 16)
-PLACE = tuple(ORDER.index(n) for n in range(BLOCKS))
+ORDER_IN = (28, 9, 19, 10, 29, 5, 7, 22, 0, 14, 8, 15, 23, 24, 21, 13, 25, 27, 6, 16, 26, 18, 11, 3, 17, 2, 1, 31, 12, 4, 30, 20)
+ORDER_OUT = (4, 12, 24, 2, 28, 10, 18, 27, 21, 9, 19, 8, 6, 17, 13, 15, 29, 3, 5, 1, 7, 14, 0, 31, 20, 30, 26, 22, 25, 11, 23, 16)
+PLACE_IN = tuple(ORDER_IN.index(n) for n in range(BLOCKS))
+PLACE_OUT = tuple(ORDER_OUT.index(n) for n in range(BLOCKS))
 PARAMS = pltpu.CompilerParams(vmem_limit_bytes=40 * 2**20)
 
 
@@ -102,7 +104,7 @@
         turned = [held[i, :, cols].astype(jnp.float32).T for i in range(3)]
         for j in range(per):
             rows = [part[2 * CH * j : 2 * CH * (j + 1)] for part in turned]
-            at = pl.ds(PLACE[block * per + j] * 6 * CH, 6 * CH)
+            at = pl.ds(PLACE_IN[block * per + j] * 6 * CH, 6 * CH)
             out_ref[at, :] = jnp.concatenate(rows).astype(jnp.bfloat16)
 
 
@@ -111,7 +113,7 @@
     copies = []
     for i, hbm in enumerate((out_hbm, grad_hbm)):
         for block in range(hbm.shape[1] // LANES):
-            spots = [(PLACE[block * rows + j] * 2 + i) * 2 * CH for j in range(rows)]
+            spots = [(PLACE_OUT[block * rows + j] * 2 + i) * 2 * CH for j in range(rows)]
             held = [in_ref[pl.ds(at, 2 * CH), :].astype(jnp.float32) for at in spots]
             part = jnp.concatenate(held).T
             made[i, :, pl.ds(block * LANES, LANES)] = part.astype(jnp.bfloat16)
@@ -183,7 +185,7 @@
         for slab in range(2):
 
             def read(n, slab=slab):
-                held = in_ref[pl.ds((PLACE[n] * 3 + a) * 2 * CH, 2 * CH), :].astype(jnp.float32)
+                held = in_ref[pl.ds((PLACE_IN[n] * 3 + a) * 2 * CH, 2 * CH), :].astype(jnp.float32)
                 return held[slab * CH : (slab + 1) * CH]
 
             made += ahead(read, cos_ref, sin_ref, work.at[a], slab)
@@ -201,7 +203,7 @@
 
     def steps(slab):
         def read(n):
-            held = in_ref[pl.ds(PLACE[n] * 2 * CH, 2 * CH), :].astype(jnp.float32)
+            held = in_ref[pl.ds(PLACE_IN[n] * 2 * CH, 2 * CH), :].astype(jnp.float32)
             return held[slab * CH : (slab + 1) * CH]
 
         return ahead(read, cos_ref, sin_ref, work.at[2], slab)
@@ -237,7 +239,7 @@
                 work[2, kept, :LANES] = part
             else:
                 both = jnp.concatenate([work[2, kept, :LANES], part])
-                out_ref[pl.ds((PLACE[n] * 2 + a) * 2 * CH, 2 * CH), :] = both.astype(jnp.bfloat16)
+                out_ref[pl.ds((PLACE_OUT[n] * 2 + a) * 2 * CH, 2 * CH), :] = both.astype(jnp.bfloat16)
 
         return dft_steps(load, 1, store)
 
@@ -252,9 +254,9 @@
     mix(back(1, 1), [])
 
 
-def exchange(rows):
+def exchange(rows, order):
     return lax.all_to_all(
-        rows, "ctx", split_axis=0, concat_axis=0, tiled=True, axis_index_groups=[list(ORDER)]
+        rows, "ctx", split_axis=0, concat_axis=0, tiled=True, axis_index_groups=[list(order)]
     )
 
 
@@ -274,7 +276,7 @@
         scratch_shapes=[pltpu.VMEM((3, LANES, chans), jnp.bfloat16), pltpu.SemaphoreType.DMA((3,))],
         compiler_params=PARAMS,
     )(*fields)
-    held = exchange(sent)
+    held = exchange(sent, ORDER_IN)
     own = held.reshape(BLOCKS, 3, 2 * CH, LANES)[:, 2].reshape(rows, LANES)
     other = lax.ppermute(own, "tp", [(i, i ^ mirror) for i in range(2 * mirror)])
     spectra = pl.pallas_call(
@@ -295,7 +297,7 @@
         compiler_params=PARAMS,
         cost_estimate=pl.CostEstimate(flops=10**9, bytes_accessed=10**6, transcendentals=0),
     )(other, spectra, cos, sin, matrices)
-    back = exchange(made)
+    back = exchange(made, ORDER_OUT)
     return pl.pallas_call(
         scatter_kernel,
         out_shape=[jax.ShapeDtypeStruct((LANES, chans), jnp.bfloat16)] * 2,

time: 65.7 us -> 65.6 us (level)
  no operation moved by 1% of the time
where the time goes in v4:
time: 65.6 us; the launch traced here: 65.4 us
  blocking collectives  53.1 us (81%)
  Pallas kernels  4.38 us (7%)
  waiting for transfers between devices  3.87 us (6%)
  starting transfers between devices  3.31 us (5%)
  between operations  0.71 us (1%)
    all_to_all x2, blocking collectives, exchange(): lax.all_to_all(rows, 'ctx', split_axis=0, concat_axis=0, tiled=True, axis...  53.1 us
    ppermute x1, waiting for transfers between devices, body(): lax.ppermute(own, 'tp', [(i, i ^ mirror) for i in range(2 * mirror)])  3.87 us
    ppermute x1, starting transfers between devices, body(): lax.ppermute(own, 'tp', [(i, i ^ mirror) for i in range(2 * mirror)])  3.31 us
  transfers between devices with their start and end apart: 1, of which 1 were waited for; matrix products, arithmetic and copies ran while one was open for 0% of the time, Pallas kernels for 2%

profile of v4, /device:TPU:6, one launch (start us, length us, event | category | flops | bytes accessed | tf_op | source)
XLA Modules:
  0.0 65.4 jit_solution(3398010429062091222)
XLA Ops:
  0.6 0.0 copy-start
  0.6 0.0 copy-start.1
  0.7 0.0 copy-start.2
  0.7 1.3 %shard_map.77 = bf16[1536,128]{1,0:T(8,128)(2,1)S(1)} custom-call(bf16[128,512]{1,0:T(8,128)(2,1)} %tok_hbm.1, bf16[128,512]{1,0:T(8,128)(2,1)} %grad_hbm.1, bf16[128,512]{1,0:T(8,128)(2,1)} %filt_hbm.1), custom_call_target="tpu_custom_call" | custom-call | tf_op jit(solution)/shard_map/pallas_call | solution.py:271
  2.0 34.2 %all_to_all.22 = bf16[32,48,128]{2,1,0:T(8,128)(2,1)S(1)} all-to-all(bf16[32,48,128]{2,1,0:T(8,128)(2,1)S(1)} %bitcast.6), channel_id=1, replica_groups={{448,144,304,160,464,80,112,352,0,224,128,240,368,384,336,208,400,432,9..., dimensions={0} | all-to-all | bytes 786432 | tf_op jit(solution)/shard_map/all_to_all | solution.py:258
  36.1 3.3 %collective-permute-start = (bf16[512,128]{1,0:T(8,128)(2,1)S(1)}, bf16[512,128]{1,0:T(8,128)(2,1)S(1)}, u32[]{:S(2)}, u32[]{:S(2)}) collective-permute-start(bf16[512,128]{1,0:T(8,128)(2,1)S(1)} %bitcast.11), channel_id=1, source_target_pairs={{0,8},{1,9},{2,10},{3,11},{4,12},{5,13},{6,14},{7,15},{8,0},{9,1},... | collective-permute-start | bytes 393224 | tf_op jit(solution)/shard_map/ppermute | solution.py:281
  39.5 0.0 copy-done
  39.5 0.0 copy-done.1
  39.5 0.0 copy-done.2
  39.5 1.1 %shard_map.78.spec = f32[3,512,256]{2,1,0:T(8,128)S(1)} custom-call(bf16[1536,128]{1,0:T(8,128)(2,1)S(1)} %bitcast.9, f32[32,128]{1,0:T(8,128)S(1)} %copy-done.2, f32[32,128]{1,0:T(8,128)S(1)} %copy-done.1, bf16[2,768,256]{2,1,0:T(8,128)(2,1)S(1)} %copy-done), custom_call_target="tpu_custom_call" | custom-call | flops 1000000000 | bytes 1000000 | tf_op jit(solution)/shard_map/pallas_call | solution.py:282
  40.6 3.9 %collective-permute-done.in_ref = bf16[512,128]{1,0:T(8,128)(2,1)S(1)} collective-permute-done((bf16[512,128]{1,0:T(8,128)(2,1)S(1)}, bf16[512,128]{1,0:T(8,128)(2,1)S(1)}, u32[]{:S(2)}, u32[]{:S(2)}) %collective-permute-start) | collective-permute-done | bytes 131104 | tf_op jit(solution)/shard_map/ppermute | solution.py:281
  44.5 1.1 %shard_map.79 = bf16[1024,128]{1,0:T(8,128)(2,1)S(1)} custom-call(bf16[512,128]{1,0:T(8,128)(2,1)S(1)} %collective-permute-done.in_ref, f32[3,512,256]{2,1,0:T(8,128)S(1)} %shard_map.78.spec, f32[32,128]{1,0:T(8,128)S(1)} %copy-done.2, f32[32,128]{1,0:T(8,128)S(1)} %copy-done.1, bf16[2,768,256]{2,1,0:T(8,128)(2,1)S(1)} %copy-done), custom_call_target="tpu_custom_call" | custom-call | flops 1000000000 | bytes 1000000 | tf_op jit(solution)/shard_map/pallas_call | solution.py:291
  45.6 19.0 %all_to_all.23 = bf16[32,32,128]{2,1,0:T(8,128)(2,1)S(1)} all-to-all(bf16[32,32,128]{2,1,0:T(8,128)(2,1)S(1)} %bitcast.10), channel_id=1, replica_groups={{64,192,384,32,448,160,288,432,336,144,304,128,96,272,208,240,464,48,80..., dimensions={0} | all-to-all | bytes 524288 | tf_op jit(solution)/shard_map/all_to_all | solution.py:258
  64.6 0.8 %shard_map.80 = (bf16[128,512]{1,0:T(8,128)(2,1)}, bf16[128,512]{1,0:T(8,128)(2,1)}) custom-call(bf16[1024,128]{1,0:T(8,128)(2,1)S(1)} %bitcast.7), custom_call_target="tpu_custom_call" | custom-call | tf_op jit(solution)/shard_map/pallas_call | solution.py:301
  (1 shorter events, 0.0 us)
Async XLA Ops:
  0.6 38.8 %copy-start = (bf16[2,768,256]{2,1,0:T(8,128)(2,1)S(1)}, bf16[2,768,256]{2,1,0:T(8,128)(2,1)}, u32[]{:S(2)}) copy-start(bf16[2,768,256]{2,1,0:T(8,128)(2,1)} %constant.8.clone.mat_ref) | copy-start | bytes 2359300
  0.6 38.8 %copy-start.1 = (f32[32,128]{1,0:T(8,128)S(1)}, f32[32,128]{1,0:T(8,128)}, u32[]{:S(2)}) copy-start(f32[32,128]{1,0:T(8,128)} %constant.7.clone.sin_ref) | copy-start | bytes 49156
  0.7 38.8 %copy-start.2 = (f32[32,128]{1,0:T(8,128)S(1)}, f32[32,128]{1,0:T(8,128)}, u32[]{:S(2)}) copy-start(f32[32,128]{1,0:T(8,128)} %constant.6.clone.cos_ref) | copy-start | bytes 49156
  36.1 8.4 %collective-permute-start = (bf16[512,128]{1,0:T(8,128)(2,1)S(1)}, bf16[512,128]{1,0:T(8,128)(2,1)S(1)}, u32[]{:S(2)}, u32[]{:S(2)}) collective-permute-start(bf16[512,128]{1,0:T(8,128)(2,1)S(1)} %bitcast.11), channel_id=1, source_target_pairs={{0,8},{1,9},{2,10},{3,11},{4,12},{5,13},{6,14},{7,15},{8,0},{9,1},... | collective-permute-start | bytes 393224 | tf_op jit(solution)/shard_map/ppermute | solution.py:281

commit v5 on v4

--- a/solution.py
+++ b/solution.py
@@ -13,7 +13,7 @@
 TOTAL = 2 * LANES * BLOCKS
 CH = 8
 PART = 128
-ORDER_IN = (28, 9, 19, 10, 29, 5, 7, 22, 0, 14, 8, 15, 23, 24, 21, 13, 25, 27, 6, 16, 26, 18, 11, 3, 17, 2, 1, 31, 12, 4, 30, 20)
+ORDER_IN = (29, 26, 10, 14, 23, 16, 17, 11, 24, 13, 20, 15, 22, 2, 7, 6, 30, 9, 19, 21, 28, 25, 18, 5, 0, 1, 27, 31, 12, 8, 3, 4)
 ORDER_OUT = (4, 12, 24, 2, 28, 10, 18, 27, 21, 9, 19, 8, 6, 17, 13, 15, 29, 3, 5, 1, 7, 14, 0, 31, 20, 30, 26, 22, 25, 11, 23, 16)
 PLACE_IN = tuple(ORDER_IN.index(n) for n in range(BLOCKS))
 PLACE_OUT = tuple(ORDER_OUT.index(n) for n in range(BLOCKS))

time: 65.6 us -> 65.1 us (level)
  no operation moved by 1% of the time
where the time goes in v5:
time: 65.1 us; the launch traced here: 64.9 us
  blocking collectives  52.6 us (81%)
  Pallas kernels  4.37 us (7%)
  waiting for transfers between devices  3.88 us (6%)
  starting transfers between devices  3.31 us (5%)
  between operations  0.71 us (1%)
    all_to_all x2, blocking collectives, exchange(): lax.all_to_all(rows, 'ctx', split_axis=0, concat_axis=0, tiled=True, axis...  52.6 us
    ppermute x1, waiting for transfers between devices, body(): lax.ppermute(own, 'tp', [(i, i ^ mirror) for i in range(2 * mirror)])  3.88 us
    ppermute x1, starting transfers between devices, body(): lax.ppermute(own, 'tp', [(i, i ^ mirror) for i in range(2 * mirror)])  3.31 us
  transfers between devices with their start and end apart: 1, of which 1 were waited for; matrix products, arithmetic and copies ran while one was open for 0% of the time, Pallas kernels for 2%

profile of v5, /device:TPU:6, one launch (start us, length us, event | category | flops | bytes accessed | tf_op | source)
XLA Modules:
  0.0 64.9 jit_solution(4792121574695753800)
XLA Ops:
  0.6 0.0 copy-start
  0.6 0.0 copy-start.1
  0.7 0.0 copy-start.2
  0.7 1.3 %shard_map.77 = bf16[1536,128]{1,0:T(8,128)(2,1)S(1)} custom-call(bf16[128,512]{1,0:T(8,128)(2,1)} %tok_hbm.1, bf16[128,512]{1,0:T(8,128)(2,1)} %grad_hbm.1, bf16[128,512]{1,0:T(8,128)(2,1)} %filt_hbm.1), custom_call_target="tpu_custom_call" | custom-call | tf_op jit(solution)/shard_map/pallas_call | solution.py:271
  2.0 33.6 %all_to_all.22 = bf16[32,48,128]{2,1,0:T(8,128)(2,1)S(1)} all-to-all(bf16[32,48,128]{2,1,0:T(8,128)(2,1)S(1)} %bitcast.6), channel_id=1, replica_groups={{464,416,160,224,368,256,272,176,384,208,320,240,352,32,112,96,480,144,..., dimensions={0} | all-to-all | bytes 786432 | tf_op jit(solution)/shard_map/all_to_all | solution.py:258
  35.6 3.3 %collective-permute-start = (bf16[512,128]{1,0:T(8,128)(2,1)S(1)}, bf16[512,128]{1,0:T(8,128)(2,1)S(1)}, u32[]{:S(2)}, u32[]{:S(2)}) collective-permute-start(bf16[512,128]{1,0:T(8,128)(2,1)S(1)} %bitcast.11), channel_id=1, source_target_pairs={{0,8},{1,9},{2,10},{3,11},{4,12},{5,13},{6,14},{7,15},{8,0},{9,1},... | collective-permute-start | bytes 393224 | tf_op jit(solution)/shard_map/ppermute | solution.py:281
  38.9 0.0 copy-done
  38.9 0.0 copy-done.1
  38.9 0.0 copy-done.2
  38.9 1.1 %shard_map.78.spec = f32[3,512,256]{2,1,0:T(8,128)S(1)} custom-call(bf16[1536,128]{1,0:T(8,128)(2,1)S(1)} %bitcast.9, f32[32,128]{1,0:T(8,128)S(1)} %copy-done.2, f32[32,128]{1,0:T(8,128)S(1)} %copy-done.1, bf16[2,768,256]{2,1,0:T(8,128)(2,1)S(1)} %copy-done), custom_call_target="tpu_custom_call" | custom-call | flops 1000000000 | bytes 1000000 | tf_op jit(solution)/shard_map/pallas_call | solution.py:282
  40.0 3.9 %collective-permute-done.in_ref = bf16[512,128]{1,0:T(8,128)(2,1)S(1)} collective-permute-done((bf16[512,128]{1,0:T(8,128)(2,1)S(1)}, bf16[512,128]{1,0:T(8,128)(2,1)S(1)}, u32[]{:S(2)}, u32[]{:S(2)}) %collective-permute-start) | collective-permute-done | bytes 131104 | tf_op jit(solution)/shard_map/ppermute | solution.py:281
  43.9 1.1 %shard_map.79 = bf16[1024,128]{1,0:T(8,128)(2,1)S(1)} custom-call(bf16[512,128]{1,0:T(8,128)(2,1)S(1)} %collective-permute-done.in_ref, f32[3,512,256]{2,1,0:T(8,128)S(1)} %shard_map.78.spec, f32[32,128]{1,0:T(8,128)S(1)} %copy-done.2, f32[32,128]{1,0:T(8,128)S(1)} %copy-done.1, bf16[2,768,256]{2,1,0:T(8,128)(2,1)S(1)} %copy-done), custom_call_target="tpu_custom_call" | custom-call | flops 1000000000 | bytes 1000000 | tf_op jit(solution)/shard_map/pallas_call | solution.py:291
  45.1 19.0 %all_to_all.23 = bf16[32,32,128]{2,1,0:T(8,128)(2,1)S(1)} all-to-all(bf16[32,32,128]{2,1,0:T(8,128)(2,1)S(1)} %bitcast.10), channel_id=1, replica_groups={{64,192,384,32,448,160,288,432,336,144,304,128,96,272,208,240,464,48,80..., dimensions={0} | all-to-all | bytes 524288 | tf_op jit(solution)/shard_map/all_to_all | solution.py:258
  64.1 0.8 %shard_map.80 = (bf16[128,512]{1,0:T(8,128)(2,1)}, bf16[128,512]{1,0:T(8,128)(2,1)}) custom-call(bf16[1024,128]{1,0:T(8,128)(2,1)S(1)} %bitcast.7), custom_call_target="tpu_custom_call" | custom-call | tf_op jit(solution)/shard_map/pallas_call | solution.py:301
  (1 shorter events, 0.0 us)
Async XLA Ops:
  0.6 38.3 %copy-start = (bf16[2,768,256]{2,1,0:T(8,128)(2,1)S(1)}, bf16[2,768,256]{2,1,0:T(8,128)(2,1)}, u32[]{:S(2)}) copy-start(bf16[2,768,256]{2,1,0:T(8,128)(2,1)} %constant.8.clone.mat_ref) | copy-start | bytes 2359300
  0.6 38.2 %copy-start.1 = (f32[32,128]{1,0:T(8,128)S(1)}, f32[32,128]{1,0:T(8,128)}, u32[]{:S(2)}) copy-start(f32[32,128]{1,0:T(8,128)} %constant.7.clone.sin_ref) | copy-start | bytes 49156
  0.7 38.2 %copy-start.2 = (f32[32,128]{1,0:T(8,128)S(1)}, f32[32,128]{1,0:T(8,128)}, u32[]{:S(2)}) copy-start(f32[32,128]{1,0:T(8,128)} %constant.6.clone.cos_ref) | copy-start | bytes 49156
  35.6 8.4 %collective-permute-start = (bf16[512,128]{1,0:T(8,128)(2,1)S(1)}, bf16[512,128]{1,0:T(8,128)(2,1)S(1)}, u32[]{:S(2)}, u32[]{:S(2)}) collective-permute-start(bf16[512,128]{1,0:T(8,128)(2,1)S(1)} %bitcast.11), channel_id=1, source_target_pairs={{0,8},{1,9},{2,10},{3,11},{4,12},{5,13},{6,14},{7,15},{8,0},{9,1},... | collective-permute-start | bytes 393224 | tf_op jit(solution)/shard_map/ppermute | solution.py:281

commit v6 on v5

--- a/solution.py
+++ b/solution.py
@@ -247,10 +247,10 @@
     mix(steps(0), [])
     mix(steps(1), inner(2, 0, 0))
     mix(multiply(0), inner(2, 1, 0))
-    mix(multiply(1), inner(0, 0, 1))
-    mix(back(0, 0), inner(0, 1, 1))
-    mix(back(0, 1), inner(1, 0, 1))
-    mix(back(1, 0), inner(1, 1, 1))
+    mix(multiply(1), inner(0, 0, 1) + inner(1, 0, 1))
+    mix(back(0, 0), inner(0, 1, 1) + inner(1, 1, 1))
+    mix(back(0, 1), [])
+    mix(back(1, 0), [])
     mix(back(1, 1), [])
 
 

time: 65.1 us -> 65.1 us (level)
  no operation moved by 1% of the time
where the time goes in v6:
time: 65.1 us; the launch traced here: 64.9 us
  blocking collectives  52.6 us (81%)
  Pallas kernels  4.34 us (7%)
  waiting for transfers between devices  3.88 us (6%)
  starting transfers between devices  3.31 us (5%)
  between operations  0.71 us (1%)
    all_to_all x2, blocking collectives, exchange(): lax.all_to_all(rows, 'ctx', split_axis=0, concat_axis=0, tiled=True, axis...  52.6 us
    ppermute x1, waiting for transfers between devices, body(): lax.ppermute(own, 'tp', [(i, i ^ mirror) for i in range(2 * mirror)])  3.88 us
    ppermute x1, starting transfers between devices, body(): lax.ppermute(own, 'tp', [(i, i ^ mirror) for i in range(2 * mirror)])  3.31 us
  transfers between devices with their start and end apart: 1, of which 1 were waited for; matrix products, arithmetic and copies ran while one was open for 0% of the time, Pallas kernels for 2%

profile of v6, /device:TPU:6, one launch (start us, length us, event | category | flops | bytes accessed | tf_op | source)
XLA Modules:
  0.0 64.9 jit_solution(1504765032864594559)
XLA Ops:
  0.6 0.0 copy-start
  0.6 0.0 copy-start.1
  0.7 0.0 copy-start.2
  0.7 1.3 %shard_map.77 = bf16[1536,128]{1,0:T(8,128)(2,1)S(1)} custom-call(bf16[128,512]{1,0:T(8,128)(2,1)} %tok_hbm.1, bf16[128,512]{1,0:T(8,128)(2,1)} %grad_hbm.1, bf16[128,512]{1,0:T(8,128)(2,1)} %filt_hbm.1), custom_call_target="tpu_custom_call" | custom-call | tf_op jit(solution)/shard_map/pallas_call | solution.py:271
  2.0 33.6 %all_to_all.22 = bf16[32,48,128]{2,1,0:T(8,128)(2,1)S(1)} all-to-all(bf16[32,48,128]{2,1,0:T(8,128)(2,1)S(1)} %bitcast.6), channel_id=1, replica_groups={{464,416,160,224,368,256,272,176,384,208,320,240,352,32,112,96,480,144,..., dimensions={0} | all-to-all | bytes 786432 | tf_op jit(solution)/shard_map/all_to_all | solution.py:258
  35.6 3.3 %collective-permute-start = (bf16[512,128]{1,0:T(8,128)(2,1)S(1)}, bf16[512,128]{1,0:T(8,128)(2,1)S(1)}, u32[]{:S(2)}, u32[]{:S(2)}) collective-permute-start(bf16[512,128]{1,0:T(8,128)(2,1)S(1)} %bitcast.11), channel_id=1, source_target_pairs={{0,8},{1,9},{2,10},{3,11},{4,12},{5,13},{6,14},{7,15},{8,0},{9,1},... | collective-permute-start | bytes 393224 | tf_op jit(solution)/shard_map/ppermute | solution.py:281
  38.9 0.0 copy-done
  38.9 0.0 copy-done.1
  38.9 0.0 copy-done.2
  38.9 1.1 %shard_map.78.spec = f32[3,512,256]{2,1,0:T(8,128)S(1)} custom-call(bf16[1536,128]{1,0:T(8,128)(2,1)S(1)} %bitcast.9, f32[32,128]{1,0:T(8,128)S(1)} %copy-done.2, f32[32,128]{1,0:T(8,128)S(1)} %copy-done.1, bf16[2,768,256]{2,1,0:T(8,128)(2,1)S(1)} %copy-done), custom_call_target="tpu_custom_call" | custom-call | flops 1000000000 | bytes 1000000 | tf_op jit(solution)/shard_map/pallas_call | solution.py:282
  40.0 3.9 %collective-permute-done.in_ref = bf16[512,128]{1,0:T(8,128)(2,1)S(1)} collective-permute-done((bf16[512,128]{1,0:T(8,128)(2,1)S(1)}, bf16[512,128]{1,0:T(8,128)(2,1)S(1)}, u32[]{:S(2)}, u32[]{:S(2)}) %collective-permute-start) | collective-permute-done | bytes 131104 | tf_op jit(solution)/shard_map/ppermute | solution.py:281
  43.9 1.1 %shard_map.79 = bf16[1024,128]{1,0:T(8,128)(2,1)S(1)} custom-call(bf16[512,128]{1,0:T(8,128)(2,1)S(1)} %collective-permute-done.in_ref, f32[3,512,256]{2,1,0:T(8,128)S(1)} %shard_map.78.spec, f32[32,128]{1,0:T(8,128)S(1)} %copy-done.2, f32[32,128]{1,0:T(8,128)S(1)} %copy-done.1, bf16[2,768,256]{2,1,0:T(8,128)(2,1)S(1)} %copy-done), custom_call_target="tpu_custom_call" | custom-call | flops 1000000000 | bytes 1000000 | tf_op jit(solution)/shard_map/pallas_call | solution.py:291
  45.0 19.0 %all_to_all.23 = bf16[32,32,128]{2,1,0:T(8,128)(2,1)S(1)} all-to-all(bf16[32,32,128]{2,1,0:T(8,128)(2,1)S(1)} %bitcast.10), channel_id=1, replica_groups={{64,192,384,32,448,160,288,432,336,144,304,128,96,272,208,240,464,48,80..., dimensions={0} | all-to-all | bytes 524288 | tf_op jit(solution)/shard_map/all_to_all | solution.py:258
  64.0 0.8 %shard_map.80 = (bf16[128,512]{1,0:T(8,128)(2,1)}, bf16[128,512]{1,0:T(8,128)(2,1)}) custom-call(bf16[1024,128]{1,0:T(8,128)(2,1)S(1)} %bitcast.7), custom_call_target="tpu_custom_call" | custom-call | tf_op jit(solution)/shard_map/pallas_call | solution.py:301
  (1 shorter events, 0.0 us)
Async XLA Ops:
  0.6 38.3 %copy-start = (bf16[2,768,256]{2,1,0:T(8,128)(2,1)S(1)}, bf16[2,768,256]{2,1,0:T(8,128)(2,1)}, u32[]{:S(2)}) copy-start(bf16[2,768,256]{2,1,0:T(8,128)(2,1)} %constant.8.clone.mat_ref) | copy-start | bytes 2359300
  0.6 38.2 %copy-start.1 = (f32[32,128]{1,0:T(8,128)S(1)}, f32[32,128]{1,0:T(8,128)}, u32[]{:S(2)}) copy-start(f32[32,128]{1,0:T(8,128)} %constant.7.clone.sin_ref) | copy-start | bytes 49156
  0.7 38.2 %copy-start.2 = (f32[32,128]{1,0:T(8,128)S(1)}, f32[32,128]{1,0:T(8,128)}, u32[]{:S(2)}) copy-start(f32[32,128]{1,0:T(8,128)} %constant.6.clone.cos_ref) | copy-start | bytes 49156
  35.6 8.4 %collective-permute-start = (bf16[512,128]{1,0:T(8,128)(2,1)S(1)}, bf16[512,128]{1,0:T(8,128)(2,1)S(1)}, u32[]{:S(2)}, u32[]{:S(2)}) collective-permute-start(bf16[512,128]{1,0:T(8,128)(2,1)S(1)} %bitcast.11), channel_id=1, source_target_pairs={{0,8},{1,9},{2,10},{3,11},{4,12},{5,13},{6,14},{7,15},{8,0},{9,1},... | collective-permute-start | bytes 393224 | tf_op jit(solution)/shard_map/ppermute | solution.py:281
